TPU v7x, 32 devices: a whole 2x2x4 slice. The times are simulated.
32 devices in a mesh: groups: 2 (over y), row: 4 (over x, core), col: 4 (over z).
Axes of the slice: x: 2, y: 2, z: 4, core: 2. Of those that a mesh axis runs over, the one named last changes fastest.
Arguments:
- pair_act: bfloat16 [320, 160, 128], P(('groups', 'row'), 'col'), parts along dimension 0, may hold values from -6 to 6
- lengths: int32 [8], P('groups'), parts along dimension 0, may hold values from 10 to 40, as said below
- in_gain: float32 [128], replicated, may hold values from 0.5 to 1.5
- in_bias: float32 [128], replicated, may hold values from -3 to 3
- w_left: bfloat16 [128, 256], replicated, may hold values from -0.5 to 0.5
- w_right: bfloat16 [128, 256], replicated, may hold values from -0.5 to 0.5
- w_gate: bfloat16 [128, 128], replicated, may hold values from -0.5 to 0.5
- mid_gain: float32 [128], replicated, may hold values from 0.5 to 1.5
- mid_bias: float32 [128], replicated, may hold values from -3 to 3
- w_out: bfloat16 [128, 128], replicated, may hold values from -0.5 to 0.5
Outputs:
- update: bfloat16 [320, 160, 128], P(('groups', 'row'), 'col'), parts along dimension 0
There are 2 independent parts, one for each index of `groups`. A program takes and returns all parts, laid end to end along the dimension named above; an argument that names none is the same for every part. Nothing has to cross between parts.
Inputs may be any that keep to these rules, and one draw needn't show every extreme that they name: lengths of chains; some chain fills all 40 positions.
All inputs are finite; a program needn't handle non-finite values.
Results may differ from a plain program's by a relative error of at most 0.0057.
Values may be sent and summed in bfloat16 or wider, within the bound.
A program may use at most 128 MiB of HBM per device.

v0:
```python
import jax
import jax.numpy as jnp
from jax import lax
from jax.sharding import PartitionSpec as P


def layer_norm(values, gain, bias):
    center = jnp.mean(values, axis=-1, keepdims=True)
    spread = jnp.mean(jnp.square(values - center), axis=-1, keepdims=True)
    return (values - center) / jnp.sqrt(spread + 1e-05) * gain + bias


def in_crop(residue_ids, lengths, slot_len):
    chain_of = residue_ids // slot_len
    chosen = chain_of[:, None] == jnp.arange(lengths.shape[0], dtype=jnp.int32)[None, :]
    chain_len = jnp.sum(jnp.where(chosen, lengths[None, :], 0), axis=1)
    return (residue_ids % slot_len < chain_len).astype(jnp.float32)


def shards(pair_act, lengths, in_gain, in_bias, w_left, w_right, w_gate, mid_gain, mid_bias, w_out):
    rows_here, cols_here, width = pair_act.shape
    hidden = w_out.shape[0]
    residues = rows_here * lax.axis_size("row")
    slot_len = residues // lengths.shape[0]
    row_ids = lax.axis_index("row") * rows_here + jnp.arange(rows_here, dtype=jnp.int32)
    col_ids = lax.axis_index("col") * cols_here + jnp.arange(cols_here, dtype=jnp.int32)
    pair_mask = (
        in_crop(row_ids, lengths, slot_len)[:, None] * in_crop(col_ids, lengths, slot_len)[None, :]
    )
    pair_norm = layer_norm(pair_act.astype(jnp.float32), in_gain, in_bias).astype(jnp.bfloat16)
    pair_norm = pair_norm.reshape(rows_here * cols_here, width)

    def edge_panel(weight):
        projected = jnp.dot(pair_norm, weight, preferred_element_type=jnp.float32)
        projected = projected.reshape(rows_here, cols_here, 2 * hidden)
        gated = (
            pair_mask[:, :, None]
            * jax.nn.sigmoid(projected[:, :, hidden:])
            * projected[:, :, :hidden]
        )
        return jnp.transpose(gated.astype(jnp.bfloat16), (2, 0, 1))

    left_edge = edge_panel(w_left)
    right_edge = edge_panel(w_right)
    partial_value = jnp.einsum(
        "hik,hjk->hij",
        left_edge,
        lax.all_gather(right_edge, "row", axis=1, tiled=True),
        preferred_element_type=jnp.float32,
    )
    triangle = lax.psum_scatter(partial_value, "col", scatter_dimension=2, tiled=True)
    triangle = jnp.transpose(triangle, (1, 2, 0))
    normed = layer_norm(triangle, mid_gain, mid_bias).astype(jnp.bfloat16)
    out_gate = jax.nn.sigmoid(jnp.dot(pair_norm, w_gate, preferred_element_type=jnp.float32))
    projected_out = jnp.dot(
        normed.reshape(rows_here * cols_here, hidden), w_out, preferred_element_type=jnp.float32
    )
    return (out_gate * projected_out).reshape(rows_here, cols_here, width).astype(jnp.bfloat16)


def solution(mesh):
    in_specs = (
        P(("groups", "row"), "col", None),
        P("groups"),
        P(),
        P(),
        P(),
        P(),
        P(),
        P(),
        P(),
        P(),
    )
    out_specs = P(("groups", "row"), "col", None)
    return jax.shard_map(shards, mesh=mesh, in_specs=in_specs, out_specs=out_specs, check_vma=False)
```

profile of v0, /device:TPU:0, one launch (start us, length us, event | category | flops | bytes accessed | tf_op | source)
XLA Modules:
  0.0 132.9 jit_solution(15936853691879364940)
XLA Ops:
  6.5 0.0 copy-start
  6.5 0.0 all-gather.2.cloned.1.call-start
  6.6 1.3 convert_reduce_fusion
  7.9 0.0 copy-start.2
  7.9 1.6 %fusion.6 = f32[40,40]{1,0:T(8,128)S(1)} fusion(bf16[40,40,128]{2,1,0:T(8,128)(2,1)} %param.10, f32[40,40]{1,0:T(8,128)S(1)} %broadcast_multiply_fusion.2), kind=kLoop, calls=%fused_computation.10 | loop fusion | flops 817600 | bytes 422400 | tf_op jit(solution)/shard_map/reduce_sum | solution.py:9
  9.5 1.5 %fusion.9 = bf16[40,40,128]{2,1,0:T(8,128)(2,1)S(1)} fusion(bf16[40,40,128]{2,1,0:T(8,128)(2,1)} %param.10, f32[128]{0:T(128)} %param.13, f32[128]{0:T(128)} %param.12, f32[40,40]{1,0:T(8,128)S(1)} %add_sqrt_fusion.1, f32[40,40]{1,0:T(8,128)S(1)} %broadcast_multiply_fusion.2), kind=kLoop, calls=%fused_computation.13 | loop fusion | flops 1228800 | bytes 833024 | tf_op jit(solution)/shard_map/convert_element_type | solution.py:30
  11.0 0.0 copy-done
  11.0 0.0 copy-start.6
  11.0 0.3 fusion.22
  11.4 0.0 copy-done.2
  11.4 0.3 fusion.24
  11.7 0.0 copy-done.6
  11.7 0.1 select_reduce_fusion.1
  11.8 0.1 broadcast_multiply_fusion
  11.9 1.2 fusion.21
  13.1 0.0 all-gather.2.cloned.1.call-update
  13.2 0.0 reduce-scatter.2.cloned.1.call-start
  13.2 1.5 %copy.20 = bf16[128,40,40]{2,1,0:T(8,128)(2,1)S(1)} copy(bf16[128,40,40]{0,2,1:T(8,128)(2,1)S(1)} %get-tuple-element.8) | data formatting | bytes 819200 | tf_op jit(solution)/shard_map/transpose | solution.py:41
  14.7 21.4 %all-gather.2.cloned.1.call-done = bf16[128,160,40]{0,2,1:T(8,128)(2,1)} async-done(((bf16[128,40,40]{0,2,1:T(8,128)(2,1)}), bf16[128,160,40]{0,2,1:T(8,128)(2,1)}) %all-gather.2.cloned.1.call-update) | async-done | bytes 1638416 | tf_op jit(solution)/shard_map/all_gather | solution.py:48
  36.0 8.7 %copy.21 = bf16[128,160,40]{2,1,0:T(8,128)(2,1)} copy(bf16[128,160,40]{0,2,1:T(8,128)(2,1)} %all-gather.2.cloned.1.call-done) | data formatting | bytes 3276800 | tf_op jit(solution)/shard_map/all_gather | solution.py:48
  44.7 8.1 %fusion.28 = f32[128,40,160]{2,1,0:T(8,128)} fusion(bf16[128,40,40]{2,1,0:T(8,128)(2,1)S(1)} %copy.20, bf16[128,160,40]{2,1,0:T(8,128)(2,1)} %copy.21), kind=kOutput, calls=%fused_computation.57 | convolution fusion | flops 65536000 | bytes 5324800 | tf_op jit(solution)/shard_map/hik,hjk->hij/dot_general | solution.py:45
  52.8 6.0 %copy.22 = f32[128,40,160]{0,1,2:T(8,128)} copy(f32[128,40,160]{2,1,0:T(8,128)} %fusion.28) | data formatting | bytes 6553600 | tf_op jit(solution)/shard_map/hik,hjk->hij/dot_general | solution.py:45
  58.8 0.0 copy-start.7
  58.8 0.0 reduce-scatter.2.cloned.1.call-update
  58.8 0.7 copy-done.7
  59.5 0.4 fusion.2
  59.9 0.0 copy-start.4
  59.9 0.0 copy-start.5
  59.9 0.0 copy-start.3
  60.0 61.3 %reduce-scatter.2.cloned.1.call-done = f32[128,40,40]{0,1,2:T(8,128)} async-done(((f32[128,40,160]{0,1,2:T(8,128)}), f32[128,40,40]{0,1,2:T(8,128)}) %reduce-scatter.2.cloned.1.call-update) | async-done | bytes 819216 | tf_op jit(solution)/shard_map/reduce_scatter | solution.py:51
  121.3 0.0 copy-start.1
  121.3 1.5 %bitcast_reduce_fusion = f32[40,40]{1,0:T(8,128)S(1)} fusion(f32[128,40,40]{0,1,2:T(8,128)} %reduce-scatter.2.cloned.1.call-done), kind=kLoop, calls=%fused_computation.29 | loop fusion | flops 203200 | bytes 825600 | tf_op jit(solution)/shard_map/reduce_sum | solution.py:8
  122.8 1.7 %multiply_reduce_fusion = f32[40,40]{1,0:T(8,128)S(1)} fusion(f32[128,40,40]{0,1,2:T(8,128)} %reduce-scatter.2.cloned.1.call-done, f32[40,40]{1,0:T(8,128)S(1)} %broadcast_multiply_fusion.1), kind=kLoop, calls=%fused_computation.31 | loop fusion | flops 612800 | bytes 832000 | tf_op jit(solution)/shard_map/reduce_sum | solution.py:9
  124.5 0.0 copy-done.4
  124.5 0.0 copy-done.5
  124.5 0.0 copy-done.1
  124.5 0.5 add_convert_fusion
  125.0 0.0 copy-done.3
  125.0 1.0 fusion.3
  (7 shorter events, 0.1 us)
Async XLA Ops:
  6.5 4.5 %copy-start = (bf16[128,256]{1,0:T(8,128)(2,1)S(1)}, bf16[128,256]{1,0:T(8,128)(2,1)}, u32[]{:S(2)}) copy-start(bf16[128,256]{1,0:T(8,128)(2,1)} %param.15) | copy-start | bytes 196612
  6.5 29.5 %all-gather.2.cloned.1.call-start = ((), (), s32[]{:S(2)}) async-start(), calls=%async_computation.1 | async-start | bytes 2048000 | tf_op jit(solution)/shard_map/all_gather | solution.py:48
  7.9 3.5 %copy-start.2 = (bf16[128,256]{1,0:T(8,128)(2,1)S(1)}, bf16[128,256]{1,0:T(8,128)(2,1)}, u32[]{:S(2)}) copy-start(bf16[128,256]{1,0:T(8,128)(2,1)} %param.14) | copy-start | bytes 196612
  11.0 0.7 copy-start.6
  13.2 108.1 %reduce-scatter.2.cloned.1.call-start = ((), (), s32[]{:S(2)}) async-start(), calls=%async_computation.2 | async-start | bytes 4096000 | tf_op jit(solution)/shard_map/reduce_scatter | solution.py:51
  58.8 0.8 copy-start.7
  59.9 64.6 %copy-start.4 = (f32[128]{0:T(128)S(1)}, f32[128]{0:T(128)}, u32[]{:S(2)}) copy-start(f32[128]{0:T(128)} %param.18) | copy-start | bytes 1540
  59.9 64.6 %copy-start.5 = (f32[128]{0:T(128)S(1)}, f32[128]{0:T(128)}, u32[]{:S(2)}) copy-start(f32[128]{0:T(128)} %param.17) | copy-start | bytes 1540
  59.9 65.1 %copy-start.3 = (bf16[128,128]{1,0:T(8,128)(2,1)S(1)}, bf16[128,128]{1,0:T(8,128)(2,1)}, u32[]{:S(2)}) copy-start(bf16[128,128]{1,0:T(8,128)(2,1)} %param.19) | copy-start | bytes 98308
  121.3 3.2 %copy-start.1 = (f32[128,40,40]{0,1,2:T(8,128)S(1)}, f32[128,40,40]{0,1,2:T(8,128)}, u32[]{:S(2)}) copy-start(f32[128,40,40]{0,1,2:T(8,128)} %reduce-scatter.2.cloned.1.call-done) | copy-start | bytes 2457604
Sparse Core Ops, SparseCore 0:
  13.3 22.7 all-gather.1
  58.9 62.2 reduce-scatter.1
where the time goes:
time: 133 us
  waiting for transfers between devices  82.7 us (62%)
  local copies, waits for them, and re-layouts  16.9 us (13%)
  between operations  13.6 us (10%)
  matrix products  10.1 us (8%)
  other arithmetic  9.47 us (7%)
    reduce_scatter x1, waiting for transfers between devices, shards(): lax.psum_scatter(partial_value, 'col', scatter_dimension=2, tiled=True)  61.3 us
    all_gather x1, waiting for transfers between devices, shards(): lax.all_gather(right_edge, 'row', axis=1, tiled=True)  21.4 us
    all_gather x1, local copies, waits for them, and re-layouts, shards(): lax.all_gather(right_edge, 'row', axis=1, tiled=True)  8.66 us
    dot_general x1, matrix products, shards(): jnp.einsum('hik,hjk->hij', left_edge, lax.all_gather(right_edge, 'row', a...  8.08 us
    dot_general x1, local copies, waits for them, and re-layouts, shards(): jnp.einsum('hik,hjk->hij', left_edge, lax.all_gather(right_edge, 'row', a...  6.01 us
    reduce_sum x2, other arithmetic, layer_norm(): spread = jnp.mean(jnp.square(values - center), axis=-1, keepdims=True)  3.21 us
    reduce_sum x2, other arithmetic, layer_norm(): center = jnp.mean(values, axis=-1, keepdims=True)  2.79 us
  transfers between devices with their start and end apart: 2, of which 2 were waited for; matrix products, arithmetic and copies ran while one was open for 1% of the time, Pallas kernels for 0%

commit v1 on v0

--- a/solution.py
+++ b/solution.py
@@ -1,6 +1,10 @@
+import functools
+
 import jax
 import jax.numpy as jnp
 from jax import lax
+from jax.experimental import pallas as pl
+from jax.experimental.pallas import tpu as pltpu
 from jax.sharding import PartitionSpec as P
 
 
@@ -17,7 +21,7 @@
     return (residue_ids % slot_len < chain_len).astype(jnp.float32)
 
 
-def shards(pair_act, lengths, in_gain, in_bias, w_left, w_right, w_gate, mid_gain, mid_bias, w_out):
+def plain_shards(pair_act, lengths, in_gain, in_bias, w_left, w_right, w_gate, mid_gain, mid_bias, w_out):
     rows_here, cols_here, width = pair_act.shape
     hidden = w_out.shape[0]
     residues = rows_here * lax.axis_size("row")
@@ -58,6 +62,290 @@
     return (out_gate * projected_out).reshape(rows_here, cols_here, width).astype(jnp.bfloat16)
 
 
+MESH = pl.DeviceIdType.MESH
+ROW, COL = 4, 4
+CHUNKS = 4
+PIECE = 4
+
+
+def half_gate(values):
+    return 0.5 * jnp.tanh(0.5 * values) + 0.5
+
+
+def fused_kernel(
+    lengths_ref, pair_ref, in_gain_ref, in_bias_ref, w_left_ref, w_right_ref, w_gate_ref,
+    mid_gain_ref, mid_bias_ref, w_out_ref, out_ref,
+    held, left_edge, right_edge, triangle, gate, got_sem, chain_sem, cross_sem,
+    *, side, slot_len,
+):
+    group, r, c = lax.axis_index("groups"), lax.axis_index("row"), lax.axis_index("col")
+    positions, width = pair_ref.shape
+    chunk = positions // CHUNKS
+    piece = PIECE * side
+    pieces = positions // piece
+    tiles = side // 8
+    chains = lengths_ref.shape[0]
+    is_source = r == c
+    same_core = r % 2 == c % 2
+    same_chip = r // 2 == c // 2
+    relays = jnp.logical_and(same_core, jnp.logical_not(same_chip))
+    sibling = r + 1 - 2 * (r % 2)
+    across = (r + 2) % ROW
+
+    def present(first, extent):
+        ids = first + lax.broadcasted_iota(jnp.int32, extent, len(extent) - 2)
+        chosen = jnp.zeros(extent, jnp.float32)
+        for chain in range(chains):
+            start = chain * slot_len
+            inside = jnp.logical_and(ids >= start, ids < start + lengths_ref[chain])
+            inside = jnp.logical_and(inside, ids < start + slot_len)
+            chosen = chosen + jnp.where(inside, 1.0, 0.0)
+        return chosen
+
+    def rows_of(part):
+        return pl.ds(pl.multiple_of(part * chunk, 16), chunk)
+
+    def transfer(source, target, part, send, device):
+        return pltpu.make_async_remote_copy(
+            src_ref=held.at[source, rows_of(part), :],
+            dst_ref=held.at[target, rows_of(part), :],
+            send_sem=send,
+            recv_sem=got_sem.at[target, part],
+            device_id=device,
+            device_id_type=MESH,
+        )
+
+    def chain_copy(k, part, way):
+        return transfer(k, k, part, chain_sem.at[k, part, way], (group, r, c + 2 * way - 1))
+
+    def cross_copy(source, k, part, way):
+        target = sibling if way == 0 else across
+        return transfer(source, COL + k, part, cross_sem.at[k, part, way], (group, target, c))
+
+    def chain_sends(k, part, finish):
+        for way in range(2):
+            fits = jnp.logical_and(k >= c, c > 0) if way == 0 else jnp.logical_and(k <= c, c < COL - 1)
+
+            @pl.when(fits)
+            def _():
+                copy = chain_copy(k, part, way)
+                copy.wait_send() if finish else copy.start()
+
+    def source_sends(k, part, finish):
+        @pl.when(is_source)
+        def _():
+            for way in (1, 0):
+                copy = cross_copy(k, k, part, way)
+                copy.wait_send() if finish else copy.start()
+
+    def relay_sends(k, part, finish):
+        @pl.when(relays)
+        def _():
+            copy = cross_copy(COL + k, k, part, 0)
+            copy.wait_send() if finish else copy.start()
+
+    def normalise(values, gain_ref, bias_ref):
+        center = jnp.mean(values, axis=-1, keepdims=True)
+        moved = values - center
+        spread = jnp.mean(jnp.square(moved), axis=-1, keepdims=True)
+        return moved * lax.rsqrt(spread + 1e-05) * gain_ref[...] + bias_ref[...]
+
+    barrier = pltpu.get_barrier_semaphore()
+    for step in range(1, ROW):
+        pl.semaphore_signal(
+            barrier, inc=1, device_id=(group, (r + step) % ROW, c), device_id_type=MESH
+        )
+
+    @pl.when(c > 0)
+    def _():
+        pl.semaphore_signal(barrier, inc=1, device_id=(group, r, c - 1), device_id_type=MESH)
+
+    @pl.when(c < COL - 1)
+    def _():
+        pl.semaphore_signal(barrier, inc=1, device_id=(group, r, c + 1), device_id_type=MESH)
+
+    def norm_piece(part):
+        rows = rows_of(part)
+        values = pair_ref[rows, :].astype(jnp.float32)
+        held[c, rows, :] = normalise(values, in_gain_ref, in_bias_ref).astype(jnp.bfloat16)
+
+    norm_piece(0)
+    pl.semaphore_wait(
+        barrier, ROW - 1 + jnp.where(c > 0, 1, 0) + jnp.where(c < COL - 1, 1, 0)
+    )
+    for part in range(CHUNKS):
+        if part > 0:
+            norm_piece(part)
+        chain_sends(c, part, False)
+        source_sends(c, part, False)
+
+    def piece_rows(t):
+        return pl.ds(pl.multiple_of(t * piece, 16), piece)
+
+    def own_piece(t, carry):
+        rows = piece_rows(t)
+        gate[rows, :] = half_gate(
+            jnp.dot(held[c, rows, :], w_gate_ref[...], preferred_element_type=jnp.float32)
+        )
+        triangle[rows, :] = jnp.zeros((piece, width), jnp.float32)
+        return carry
+
+    lax.fori_loop(0, pieces, own_piece, 0)
+
+    def edge(slot, weight_ref, rows):
+        projected = jnp.dot(
+            held[slot, rows, :], weight_ref[...], preferred_element_type=jnp.float32
+        )
+        return projected[:, :width] * half_gate(projected[:, width:])
+
+    def left_part(k):
+        def left_piece(t, carry):
+            rows = piece_rows(t)
+            left_edge[rows, :] = edge(k, w_left_ref, rows)
+            return carry
+
+        lax.fori_loop(0, pieces, left_piece, 0)
+
+    def right_part(k):
+        slot = jnp.where(is_source, k, COL + k)
+        mask_k = present(k * side, (side, width))
+
+        def right_piece(t, carry):
+            rows = piece_rows(t)
+            value = edge(slot, w_right_ref, rows).reshape(PIECE, side, width) * mask_k[None]
+            right_edge[rows, :] = value.reshape(piece, width)
+            return carry
+
+        lax.fori_loop(0, pieces, right_piece, 0)
+
+    def multiply():
+        def some_rows(block, carry):
+            base = pl.multiple_of(block * (8 * side), 8)
+
+            def add_k(k, sums):
+                rights = [
+                    right_edge[pl.ds(tile * 8 * side + k, 8, stride=side), :]
+                    for tile in range(tiles)
+                ]
+                new = []
+                for i in range(8):
+                    left = left_edge[pl.ds(base + i * side + k, 1), :]
+                    for tile in range(tiles):
+                        new.append(sums[i * tiles + tile] + left * rights[tile])
+                return tuple(new)
+
+            where = [
+                pl.ds(pl.multiple_of(base + i * side + tile * 8, 8), 8)
+                for i in range(8)
+                for tile in range(tiles)
+            ]
+            sums = tuple(triangle[rows, :] for rows in where)
+            sums = lax.fori_loop(0, side, add_k, sums, unroll=4)
+            for rows, value in zip(where, sums):
+                triangle[rows, :] = value
+            return carry
+
+        lax.fori_loop(0, side // 8, some_rows, 0)
+
+    def at_distance(distance, act):
+        for sign in (-1, 1) if distance > 0 else (1,):
+            k = c + sign * distance
+
+            @pl.when(jnp.logical_and(k >= 0, k < COL))
+            def _():
+                act(k)
+
+    def gather(distance):
+        def pass_on(part, carry):
+            def act(k):
+                chain_copy(k, part, 0).wait_recv()
+                chain_sends(k, part, False)
+                source_sends(k, part, False)
+
+            at_distance(distance, act)
+            return carry
+
+        lax.fori_loop(0, CHUNKS, pass_on, 0)
+
+    def receive_right(k):
+        @pl.when(jnp.logical_not(is_source))
+        def _():
+            def pass_on(part, carry):
+                cross_copy(k, k, part, 0).wait_recv()
+                relay_sends(k, part, False)
+                return carry
+
+            lax.fori_loop(0, CHUNKS, pass_on, 0)
+
+    def work(k):
+        left_part(k)
+        receive_right(k)
+        right_part(k)
+        multiply()
+
+    for distance in range(1, COL):
+        gather(distance)
+        at_distance(distance - 1, work)
+    at_distance(COL - 1, work)
+
+    mask_j = present(c * side, (side, width))
+
+    def finish_piece(t, carry):
+        rows = piece_rows(t)
+        parts = []
+        for i in range(PIECE):
+            mask_i = present(r * side + t * PIECE + i, (1, width))
+            parts.append(mask_i * mask_j)
+        mask = jnp.concatenate(parts, axis=0)
+        normed = normalise(triangle[rows, :] * mask, mid_gain_ref, mid_bias_ref)
+        projected = jnp.dot(
+            normed.astype(jnp.bfloat16), w_out_ref[...], preferred_element_type=jnp.float32
+        )
+        out_ref[rows, :] = (gate[rows, :] * projected).astype(out_ref.dtype)
+        return carry
+
+    lax.fori_loop(0, pieces, finish_piece, 0)
+
+    def drain(index, carry):
+        k, part = index // CHUNKS, index % CHUNKS
+        chain_sends(k, part, True)
+        source_sends(k, part, True)
+        relay_sends(k, part, True)
+        return carry
+
+    lax.fori_loop(0, COL * CHUNKS, drain, 0)
+
+
+def fused_shards(pair_act, lengths, in_gain, in_bias, w_left, w_right, w_gate, mid_gain, mid_bias, w_out):
+    side, _, width = pair_act.shape
+    positions = side * side
+    slot_len = side * ROW // lengths.shape[0]
+    vmem = pl.BlockSpec(memory_space=pltpu.VMEM)
+    out = pl.pallas_call(
+        functools.partial(fused_kernel, side=side, slot_len=slot_len),
+        out_shape=jax.ShapeDtypeStruct((positions, width), jnp.bfloat16),
+        in_specs=[pl.BlockSpec(memory_space=pltpu.SMEM)] + [vmem] * 9,
+        out_specs=vmem,
+        scratch_shapes=[
+            pltpu.VMEM((2 * COL, positions, width), jnp.bfloat16),
+            pltpu.VMEM((positions, width), jnp.float32),
+            pltpu.VMEM((positions, width), jnp.float32),
+            pltpu.VMEM((positions, width), jnp.float32),
+            pltpu.VMEM((positions, width), jnp.float32),
+            pltpu.SemaphoreType.DMA((2 * COL, CHUNKS)),
+            pltpu.SemaphoreType.DMA((COL, CHUNKS, 2)),
+            pltpu.SemaphoreType.DMA((COL, CHUNKS, 2)),
+        ],
+        compiler_params=pltpu.CompilerParams(
+            collective_id=0, has_side_effects=True, vmem_limit_bytes=32 * 1024 * 1024
+        ),
+    )(
+        lengths, pair_act.reshape(positions, width), in_gain[None], in_bias[None], w_left, w_right,
+        w_gate, mid_gain[None], mid_bias[None], w_out,
+    )
+    return out.reshape(side, side, width)
+
+
 def solution(mesh):
     in_specs = (
         P(("groups", "row"), "col", None),
@@ -72,4 +360,7 @@
         P(),
     )
     out_specs = P(("groups", "row"), "col", None)
+    shards = plain_shards
+    if mesh.shape["row"] == 4 and mesh.shape["col"] == 4:
+        shards = fused_shards
     return jax.shard_map(shards, mesh=mesh, in_specs=in_specs, out_specs=out_specs, check_vma=False)

time: 133 us -> 55.8 us (0.42)
  waiting for transfers between devices: 82.7 us -> 0 us
  Pallas kernels: 0 us -> 49.7 us
  between operations: 13.6 us -> 0.02 us
  local copies, waits for them, and re-layouts: 16.9 us -> 5.66 us
  matrix products: 10.1 us -> 0 us
  other arithmetic: 9.47 us -> 0 us
    reduce_scatter x1 -> x0, waiting for transfers between devices: 61.3 us -> none  [shards(): lax.psum_scatter(partial_value, 'col', scatter_dimension=2, tiled=True)]
    pallas_call x0 -> x1, Pallas kernels: none -> 49.7 us  [fused_shards(): pl.pallas_call(functools.partial(fused_kernel, side=side, slot_len=slot_l...]
    all_gather x1 -> x0, waiting for transfers between devices: 21.4 us -> none  [shards(): lax.all_gather(right_edge, 'row', axis=1, tiled=True)]
    dot_general x5 -> x0, matrix products: 10.1 us -> none  [the longest x1 8.08 us: shards(): jnp.einsum('hik,hjk->hij', left_edge, lax.all_gather(right_edge, 'row', a...]
    all_gather x1 -> x0, local copies, waits for them, and re-layouts: 8.66 us -> none  [shards(): lax.all_gather(right_edge, 'row', axis=1, tiled=True)]
    reduce_sum x5 -> x0, other arithmetic: 6.09 us -> none  [the longest x2 3.21 us: layer_norm(): spread = jnp.mean(jnp.square(values - center), axis=-1, keepdims=True)]
    dot_general x1 -> x0, local copies, waits for them, and re-layouts: 6.01 us -> none  [shards(): jnp.einsum('hik,hjk->hij', left_edge, lax.all_gather(right_edge, 'row', a...]
    unnamed x16 -> x21, local copies, waits for them, and re-layouts: 0.77 us -> 5.66 us
  transfers between devices with their start and end apart: 2 -> 0, of which waited for: 2 -> 0; matrix products, arithmetic and copies ran while one was open for 1% -> 0% of each run, Pallas kernels for 0% -> 0%
where the time goes in v1:
time: 55.8 us; the launch traced here: 55.3 us
  Pallas kernels  49.7 us (89%)
  local copies, waits for them, and re-layouts  5.66 us (10%)
    pallas_call x1, Pallas kernels, fused_shards(): pl.pallas_call(functools.partial(fused_kernel, side=side, slot_len=slot_l...  49.7 us
    unnamed x21, local copies, waits for them, and re-layouts  5.66 us

profile of v1, /device:TPU:0, one launch (start us, length us, event | category | flops | bytes accessed | tf_op | source)
XLA Modules:
  0.0 55.3 jit_solution(4124368775835698190)
XLA Ops:
  0.0 0.0 copy-start.8
  0.0 0.0 copy-start.9
  0.0 0.0 copy-start.5
  0.0 0.0 copy-start.6
  0.0 0.0 copy-start.7
  0.0 0.6 %copy-done.8 = f32[128]{0:T(128)S(1)} copy-done((f32[128]{0:T(128)S(1)}, f32[128]{0:T(128)}, u32[]{:S(2)}) %copy-start.8) | copy-done | bytes 536
  0.7 0.0 copy-done.9
  0.7 0.0 copy-done.5
  0.7 0.0 copy-done.6
  0.7 0.0 copy-done.7
  0.7 0.0 copy-start
  0.7 1.0 %copy-done = bf16[40,40,128]{2,1,0:T(8,128)(2,1)S(1)} copy-done((bf16[40,40,128]{2,1,0:T(8,128)(2,1)S(1)}, bf16[40,40,128]{2,1,0:T(8,128)(2,1)}, u32[]{:S(2)}) %copy-start) | copy-done | bytes 409624
  1.7 0.0 copy-start.1
  1.7 0.8 %copy-done.1 = bf16[128,256]{1,0:T(8,128)(2,1)S(1)} copy-done((bf16[128,256]{1,0:T(8,128)(2,1)S(1)}, bf16[128,256]{1,0:T(8,128)(2,1)}, u32[]{:S(2)}) %copy-start.1) | copy-done | bytes 65560
  2.6 0.0 copy-start.2
  2.6 0.8 %copy-done.2 = bf16[128,256]{1,0:T(8,128)(2,1)S(1)} copy-done((bf16[128,256]{1,0:T(8,128)(2,1)S(1)}, bf16[128,256]{1,0:T(8,128)(2,1)}, u32[]{:S(2)}) %copy-start.2) | copy-done | bytes 65560
  3.4 0.0 copy-start.3
  3.4 0.8 %copy-done.3 = bf16[128,128]{1,0:T(8,128)(2,1)S(1)} copy-done((bf16[128,128]{1,0:T(8,128)(2,1)S(1)}, bf16[128,128]{1,0:T(8,128)(2,1)}, u32[]{:S(2)}) %copy-start.3) | copy-done | bytes 32792
  4.2 0.0 copy-start.4
  4.2 0.8 %copy-done.4 = bf16[128,128]{1,0:T(8,128)(2,1)S(1)} copy-done((bf16[128,128]{1,0:T(8,128)(2,1)S(1)}, bf16[128,128]{1,0:T(8,128)(2,1)}, u32[]{:S(2)}) %copy-start.4) | copy-done | bytes 32792
  4.9 49.7 %shard_map.100 = bf16[1600,128]{1,0:T(8,128)(2,1)S(1)} custom-call(s32[4]{0:T(128)S(1)} %copy-done.5, bf16[1600,128]{1,0:T(8,128)(2,1)S(1)} %bitcast.7, f32[1,128]{1,0:T(1,128)S(1)} %bitcast.8, f32[1,128]{1,0:T(1,128)S(1)} %bitcast.9, bf16[128,256]{1,0:T(8,128)(2,1)S(1)} %copy-done.1, bf16[128,256]{1,0:T(8,128)(2,1)S(1)} %copy-done.2, ...), custom_call_target="tpu_custom_call" | custom-call | tf_op jit(solution)/shard_map/pallas_call | solution.py:324
  54.6 0.8 %copy.12 = bf16[40,40,128]{2,1,0:T(8,128)(2,1)} copy(bf16[40,40,128]{2,1,0:T(8,128)(2,1)S(1)} %bitcast.6) | data formatting | bytes 819200
Async XLA Ops:
  0.0 0.7 %copy-start.8 = (f32[128]{0:T(128)S(1)}, f32[128]{0:T(128)}, u32[]{:S(2)}) copy-start(f32[128]{0:T(128)} %param.17) | copy-start | bytes 1540
  0.0 0.7 %copy-start.9 = (f32[128]{0:T(128)S(1)}, f32[128]{0:T(128)}, u32[]{:S(2)}) copy-start(f32[128]{0:T(128)} %param.18) | copy-start | bytes 1540
  0.0 0.7 %copy-start.5 = (s32[4]{0:T(128)S(1)}, s32[4]{0:T(128)}, u32[]{:S(2)}) copy-start(s32[4]{0:T(128)} %lengths_ref.1) | copy-start | bytes 52
  0.0 0.7 %copy-start.6 = (f32[128]{0:T(128)S(1)}, f32[128]{0:T(128)}, u32[]{:S(2)}) copy-start(f32[128]{0:T(128)} %param.12) | copy-start | bytes 1540
  0.0 0.7 %copy-start.7 = (f32[128]{0:T(128)S(1)}, f32[128]{0:T(128)}, u32[]{:S(2)}) copy-start(f32[128]{0:T(128)} %param.13) | copy-start | bytes 1540
  0.7 1.0 %copy-start = (bf16[40,40,128]{2,1,0:T(8,128)(2,1)S(1)}, bf16[40,40,128]{2,1,0:T(8,128)(2,1)}, u32[]{:S(2)}) copy-start(bf16[40,40,128]{2,1,0:T(8,128)(2,1)} %param.10) | copy-start | bytes 1228804
  1.7 0.8 %copy-start.1 = (bf16[128,256]{1,0:T(8,128)(2,1)S(1)}, bf16[128,256]{1,0:T(8,128)(2,1)}, u32[]{:S(2)}) copy-start(bf16[128,256]{1,0:T(8,128)(2,1)} %w_left_ref.1) | copy-start | bytes 196612
  2.6 0.8 %copy-start.2 = (bf16[128,256]{1,0:T(8,128)(2,1)S(1)}, bf16[128,256]{1,0:T(8,128)(2,1)}, u32[]{:S(2)}) copy-start(bf16[128,256]{1,0:T(8,128)(2,1)} %w_right_ref.1) | copy-start | bytes 196612
  3.4 0.8 %copy-start.3 = (bf16[128,128]{1,0:T(8,128)(2,1)S(1)}, bf16[128,128]{1,0:T(8,128)(2,1)}, u32[]{:S(2)}) copy-start(bf16[128,128]{1,0:T(8,128)(2,1)} %w_gate_ref.1) | copy-start | bytes 98308
  4.2 0.8 %copy-start.4 = (bf16[128,128]{1,0:T(8,128)(2,1)S(1)}, bf16[128,128]{1,0:T(8,128)(2,1)}, u32[]{:S(2)}) copy-start(bf16[128,128]{1,0:T(8,128)(2,1)} %w_out_ref.1) | copy-start | bytes 98308

commit v2 on v1

--- a/solution.py
+++ b/solution.py
@@ -64,8 +64,8 @@
 
 MESH = pl.DeviceIdType.MESH
 ROW, COL = 4, 4
-CHUNKS = 4
-PIECE = 4
+CHUNKS = 2
+PIECE = 40
 
 
 def half_gate(values):
@@ -73,9 +73,10 @@
 
 
 def fused_kernel(
+    lengths_hbm, pair_hbm, in_gain_hbm, in_bias_hbm, w_left_hbm, w_right_hbm, w_gate_hbm,
+    mid_gain_hbm, mid_bias_hbm, w_out_hbm, out_ref,
     lengths_ref, pair_ref, in_gain_ref, in_bias_ref, w_left_ref, w_right_ref, w_gate_ref,
-    mid_gain_ref, mid_bias_ref, w_out_ref, out_ref,
-    held, left_edge, right_edge, triangle, gate, got_sem, chain_sem, cross_sem,
+    mid_gain_ref, mid_bias_ref, w_out_ref, load_sem, held, left_edge, right_edge, triangle, gate, got_sem, chain_sem, cross_sem,
     *, side, slot_len,
 ):
     group, r, c = lax.axis_index("groups"), lax.axis_index("row"), lax.axis_index("col")
@@ -150,6 +151,17 @@
         spread = jnp.mean(jnp.square(moved), axis=-1, keepdims=True)
         return moved * lax.rsqrt(spread + 1e-05) * gain_ref[...] + bias_ref[...]
 
+    loads = [
+        pltpu.make_async_copy(source, target, load_sem.at[index])
+        for index, (source, target) in enumerate((
+            (pair_hbm, pair_ref), (in_gain_hbm, in_gain_ref), (in_bias_hbm, in_bias_ref),
+            (w_gate_hbm, w_gate_ref), (w_left_hbm, w_left_ref), (lengths_hbm, lengths_ref),
+            (w_right_hbm, w_right_ref), (mid_gain_hbm, mid_gain_ref),
+            (mid_bias_hbm, mid_bias_ref), (w_out_hbm, w_out_ref),
+        ))
+    ]
+    for load in loads:
+        load.start()
     barrier = pltpu.get_barrier_semaphore()
     for step in range(1, ROW):
         pl.semaphore_signal(
@@ -169,6 +181,8 @@
         values = pair_ref[rows, :].astype(jnp.float32)
         held[c, rows, :] = normalise(values, in_gain_ref, in_bias_ref).astype(jnp.bfloat16)
 
+    for load in loads[:3]:
+        load.wait()
     norm_piece(0)
     pl.semaphore_wait(
         barrier, ROW - 1 + jnp.where(c > 0, 1, 0) + jnp.where(c < COL - 1, 1, 0)
@@ -178,6 +192,9 @@
             norm_piece(part)
         chain_sends(c, part, False)
         source_sends(c, part, False)
+
+    for load in loads[3:]:
+        load.wait()
 
     def piece_rows(t):
         return pl.ds(pl.multiple_of(t * piece, 16), piece)
@@ -240,7 +257,7 @@
                 for tile in range(tiles)
             ]
             sums = tuple(triangle[rows, :] for rows in where)
-            sums = lax.fori_loop(0, side, add_k, sums, unroll=4)
+            sums = lax.fori_loop(0, side, add_k, sums, unroll=8)
             for rows, value in zip(where, sums):
                 triangle[rows, :] = value
             return carry
@@ -248,12 +265,17 @@
         lax.fori_loop(0, side // 8, some_rows, 0)
 
     def at_distance(distance, act):
-        for sign in (-1, 1) if distance > 0 else (1,):
-            k = c + sign * distance
-
-            @pl.when(jnp.logical_and(k >= 0, k < COL))
+        def on_side(sign, carry):
+            k = c + (2 * sign - 1) * distance
+            inside = jnp.logical_and(k >= 0, k < COL)
+
+            @pl.when(jnp.logical_and(inside, jnp.logical_or(distance > 0, sign > 0)))
             def _():
                 act(k)
+
+            return carry
+
+        lax.fori_loop(0, 2, on_side, 0)
 
     def gather(distance):
         def pass_on(part, carry):
@@ -283,10 +305,15 @@
         right_part(k)
         multiply()
 
-    for distance in range(1, COL):
-        gather(distance)
+    def stage(distance, carry):
+        @pl.when(distance < COL)
+        def _():
+            gather(distance)
+
         at_distance(distance - 1, work)
-    at_distance(COL - 1, work)
+        return carry
+
+    lax.fori_loop(1, COL + 1, stage, 0)
 
     mask_j = present(c * side, (side, width))
 
@@ -324,9 +351,20 @@
     out = pl.pallas_call(
         functools.partial(fused_kernel, side=side, slot_len=slot_len),
         out_shape=jax.ShapeDtypeStruct((positions, width), jnp.bfloat16),
-        in_specs=[pl.BlockSpec(memory_space=pltpu.SMEM)] + [vmem] * 9,
+        in_specs=[pl.BlockSpec(memory_space=pltpu.HBM)] * 10,
         out_specs=vmem,
         scratch_shapes=[
+            pltpu.SMEM(lengths.shape, jnp.int32),
+            pltpu.VMEM((positions, width), jnp.bfloat16),
+            pltpu.VMEM((1, width), jnp.float32),
+            pltpu.VMEM((1, width), jnp.float32),
+            pltpu.VMEM(w_left.shape, jnp.bfloat16),
+            pltpu.VMEM(w_right.shape, jnp.bfloat16),
+            pltpu.VMEM(w_gate.shape, jnp.bfloat16),
+            pltpu.VMEM((1, width), jnp.float32),
+            pltpu.VMEM((1, width), jnp.float32),
+            pltpu.VMEM(w_out.shape, jnp.bfloat16),
+            pltpu.SemaphoreType.DMA((10,)),
             pltpu.VMEM((2 * COL, positions, width), jnp.bfloat16),
             pltpu.VMEM((positions, width), jnp.float32),
             pltpu.VMEM((positions, width), jnp.float32),
@@ -337,7 +375,7 @@
             pltpu.SemaphoreType.DMA((COL, CHUNKS, 2)),
         ],
         compiler_params=pltpu.CompilerParams(
-            collective_id=0, has_side_effects=True, vmem_limit_bytes=32 * 1024 * 1024
+            collective_id=0, has_side_effects=True, vmem_limit_bytes=56 * 1024 * 1024
         ),
     )(
         lengths, pair_act.reshape(positions, width), in_gain[None], in_bias[None], w_left, w_right,

time: 55.8 us -> 43.7 us (0.78)
  Pallas kernels: 49.7 us -> 41.7 us
  local copies, waits for them, and re-layouts: 5.66 us -> 1.79 us
    pallas_call x1, Pallas kernels: 49.7 us -> 41.7 us  [fused_shards(): pl.pallas_call(functools.partial(fused_kernel, side=side, slot_len=slot_l...]
    unnamed x21 -> x1, local copies, waits for them, and re-layouts: 5.66 us -> 1.79 us
where the time goes in v2:
time: 43.7 us; the launch traced here: 43.5 us
  Pallas kernels  41.7 us (95%)
  local copies, waits for them, and re-layouts  1.79 us (4%)
    pallas_call x1, Pallas kernels, fused_shards(): pl.pallas_call(functools.partial(fused_kernel, side=side, slot_len=slot_l...  41.7 us
    unnamed x1, local copies, waits for them, and re-layouts  1.79 us

profile of v2, /device:TPU:0, one launch (start us, length us, event | category | flops | bytes accessed | tf_op | source)
XLA Modules:
  0.0 43.5 jit_solution(667843411717619698)
XLA Ops:
  0.0 41.7 %shard_map.100 = bf16[1600,128]{1,0:T(8,128)(2,1)} custom-call(s32[4]{0:T(128)} %lengths_hbm.1, bf16[1600,128]{1,0:T(8,128)(2,1)} %bitcast.7, f32[1,128]{1,0:T(1,128)} %bitcast.8, f32[1,128]{1,0:T(1,128)} %bitcast.9, bf16[128,256]{1,0:T(8,128)(2,1)} %w_left_hbm.1, bf16[128,256]{1,0:T(8,128)(2,1)} %w_right_hbm.1, bf16[128,128]{1,0:T(8,128)(2,1)} %w_gate_hbm.1, ...), custom_call_target="tpu_custom_call" | custom-call | tf_op jit(solution)/shard_map/pallas_call | solution.py:351
  41.8 1.8 %copy.12 = bf16[40,40,128]{2,1,0:T(8,128)(2,1)} copy(bf16[40,40,128]{2,1,0:T(8,128)(2,1)} %bitcast.6) | data formatting | bytes 819200

commit v3 on v2

--- a/solution.py
+++ b/solution.py
@@ -64,7 +64,7 @@
 
 MESH = pl.DeviceIdType.MESH
 ROW, COL = 4, 4
-CHUNKS = 2
+CHUNKS = 5
 PIECE = 40
 
 
@@ -223,46 +223,29 @@
 
         lax.fori_loop(0, pieces, left_piece, 0)
 
-    def right_part(k):
+    tile_rows = positions // tiles
+
+    def right_tile(k, tile):
         slot = jnp.where(is_source, k, COL + k)
         mask_k = present(k * side, (side, width))
-
-        def right_piece(t, carry):
-            rows = piece_rows(t)
-            value = edge(slot, w_right_ref, rows).reshape(PIECE, side, width) * mask_k[None]
-            right_edge[rows, :] = value.reshape(piece, width)
-            return carry
-
-        lax.fori_loop(0, pieces, right_piece, 0)
-
-    def multiply():
-        def some_rows(block, carry):
-            base = pl.multiple_of(block * (8 * side), 8)
-
-            def add_k(k, sums):
-                rights = [
-                    right_edge[pl.ds(tile * 8 * side + k, 8, stride=side), :]
-                    for tile in range(tiles)
-                ]
-                new = []
-                for i in range(8):
-                    left = left_edge[pl.ds(base + i * side + k, 1), :]
-                    for tile in range(tiles):
-                        new.append(sums[i * tiles + tile] + left * rights[tile])
-                return tuple(new)
-
-            where = [
-                pl.ds(pl.multiple_of(base + i * side + tile * 8, 8), 8)
-                for i in range(8)
-                for tile in range(tiles)
-            ]
-            sums = tuple(triangle[rows, :] for rows in where)
-            sums = lax.fori_loop(0, side, add_k, sums, unroll=8)
-            for rows, value in zip(where, sums):
-                triangle[rows, :] = value
-            return carry
-
-        lax.fori_loop(0, side // 8, some_rows, 0)
+        rows = pl.ds(pl.multiple_of(tile * tile_rows, 16), tile_rows)
+        value = edge(slot, w_right_ref, rows).reshape(8, side, width) * mask_k[None]
+        right_edge[...] = value.reshape(tile_rows, width)
+
+        def add_k(k, sums):
+            right = right_edge[pl.ds(k, 8, stride=side), :]
+            return tuple(
+                total + left_edge[pl.ds(i * side + k, 1), :] * right
+                for i, total in enumerate(sums)
+            )
+
+        where = [
+            pl.ds(pl.multiple_of(i * side + tile * 8, 8), 8) for i in range(side)
+        ]
+        sums = tuple(triangle[rows, :] for rows in where)
+        sums = lax.fori_loop(0, side, add_k, sums, unroll=8)
+        for rows, value in zip(where, sums):
+            triangle[rows, :] = value
 
     def at_distance(distance, act):
         def on_side(sign, carry):
@@ -289,31 +272,35 @@
 
         lax.fori_loop(0, CHUNKS, pass_on, 0)
 
-    def receive_right(k):
-        @pl.when(jnp.logical_not(is_source))
-        def _():
-            def pass_on(part, carry):
+    def work(k):
+        left_part(k)
+
+        def each_tile(part, carry):
+            @pl.when(jnp.logical_not(is_source))
+            def _():
                 cross_copy(k, k, part, 0).wait_recv()
                 relay_sends(k, part, False)
-                return carry
-
-            lax.fori_loop(0, CHUNKS, pass_on, 0)
-
-    def work(k):
-        left_part(k)
-        receive_right(k)
-        right_part(k)
-        multiply()
+
+            right_tile(k, part)
+            return carry
+
+        lax.fori_loop(0, CHUNKS, each_tile, 0)
+
+    at_end = jnp.logical_or(c == 0, c == COL - 1)
 
     def stage(distance, carry):
-        @pl.when(distance < COL)
+        early = jnp.where(distance < 2, distance + 1, 0)
+        late = jnp.where(distance == 0, 1, jnp.where(distance == 1, 0, distance))
+        next_gather = jnp.where(at_end, late, early)
+
+        @pl.when(next_gather > 0)
         def _():
-            gather(distance)
-
-        at_distance(distance - 1, work)
+            gather(next_gather)
+
+        at_distance(distance, work)
         return carry
 
-    lax.fori_loop(1, COL + 1, stage, 0)
+    lax.fori_loop(0, COL, stage, 0)
 
     mask_j = present(c * side, (side, width))
 
@@ -367,7 +354,7 @@
             pltpu.SemaphoreType.DMA((10,)),
             pltpu.VMEM((2 * COL, positions, width), jnp.bfloat16),
             pltpu.VMEM((positions, width), jnp.float32),
-            pltpu.VMEM((positions, width), jnp.float32),
+            pltpu.VMEM((8 * side, width), jnp.float32),
             pltpu.VMEM((positions, width), jnp.float32),
             pltpu.VMEM((positions, width), jnp.float32),
             pltpu.SemaphoreType.DMA((2 * COL, CHUNKS)),

time: 43.7 us -> 40.9 us (0.936)
  Pallas kernels: 41.7 us -> 39 us
    pallas_call x1, Pallas kernels: 41.7 us -> 39 us  [fused_shards(): pl.pallas_call(functools.partial(fused_kernel, side=side, slot_len=slot_l...]
where the time goes in v3:
time: 40.9 us; the launch traced here: 40.8 us
  Pallas kernels  39 us (95%)
  local copies, waits for them, and re-layouts  1.79 us (4%)
    pallas_call x1, Pallas kernels, fused_shards(): pl.pallas_call(functools.partial(fused_kernel, side=side, slot_len=slot_l...  39 us
    unnamed x1, local copies, waits for them, and re-layouts  1.79 us

profile of v3, /device:TPU:0, one launch (start us, length us, event | category | flops | bytes accessed | tf_op | source)
XLA Modules:
  0.0 40.8 jit_solution(6180431984330173487)
XLA Ops:
  0.0 39.0 %shard_map.100 = bf16[1600,128]{1,0:T(8,128)(2,1)} custom-call(s32[4]{0:T(128)} %lengths_hbm.1, bf16[1600,128]{1,0:T(8,128)(2,1)} %bitcast.7, f32[1,128]{1,0:T(1,128)} %bitcast.8, f32[1,128]{1,0:T(1,128)} %bitcast.9, bf16[128,256]{1,0:T(8,128)(2,1)} %w_left_hbm.1, bf16[128,256]{1,0:T(8,128)(2,1)} %w_right_hbm.1, bf16[128,128]{1,0:T(8,128)(2,1)} %w_gate_hbm.1, ...), custom_call_target="tpu_custom_call" | custom-call | tf_op jit(solution)/shard_map/pallas_call | solution.py:338
  39.0 1.8 %copy.12 = bf16[40,40,128]{2,1,0:T(8,128)(2,1)} copy(bf16[40,40,128]{2,1,0:T(8,128)(2,1)} %bitcast.6) | data formatting | bytes 819200

commit v4 on v3

--- a/solution.py
+++ b/solution.py
@@ -76,7 +76,7 @@
     lengths_hbm, pair_hbm, in_gain_hbm, in_bias_hbm, w_left_hbm, w_right_hbm, w_gate_hbm,
     mid_gain_hbm, mid_bias_hbm, w_out_hbm, out_ref,
     lengths_ref, pair_ref, in_gain_ref, in_bias_ref, w_left_ref, w_right_ref, w_gate_ref,
-    mid_gain_ref, mid_bias_ref, w_out_ref, load_sem, held, left_edge, right_edge, triangle, gate, got_sem, chain_sem, cross_sem,
+    mid_gain_ref, mid_bias_ref, w_out_ref, load_sem, pair_sem, held, left_edge, right_edge, triangle, gate, got_sem, chain_sem, cross_sem,
     *, side, slot_len,
 ):
     group, r, c = lax.axis_index("groups"), lax.axis_index("row"), lax.axis_index("col")
@@ -154,13 +154,19 @@
     loads = [
         pltpu.make_async_copy(source, target, load_sem.at[index])
         for index, (source, target) in enumerate((
-            (pair_hbm, pair_ref), (in_gain_hbm, in_gain_ref), (in_bias_hbm, in_bias_ref),
+            (in_gain_hbm, in_gain_ref), (in_bias_hbm, in_bias_ref),
             (w_gate_hbm, w_gate_ref), (w_left_hbm, w_left_ref), (lengths_hbm, lengths_ref),
             (w_right_hbm, w_right_ref), (mid_gain_hbm, mid_gain_ref),
             (mid_bias_hbm, mid_bias_ref), (w_out_hbm, w_out_ref),
         ))
     ]
-    for load in loads:
+    pair_loads = [
+        pltpu.make_async_copy(
+            pair_hbm.at[rows_of(part), :], pair_ref.at[rows_of(part), :], pair_sem.at[part]
+        )
+        for part in range(CHUNKS)
+    ]
+    for load in loads[:2] + pair_loads + loads[2:]:
         load.start()
     barrier = pltpu.get_barrier_semaphore()
     for step in range(1, ROW):
@@ -181,19 +187,21 @@
         values = pair_ref[rows, :].astype(jnp.float32)
         held[c, rows, :] = normalise(values, in_gain_ref, in_bias_ref).astype(jnp.bfloat16)
 
-    for load in loads[:3]:
+    for load in loads[:2]:
         load.wait()
+    pair_loads[0].wait()
     norm_piece(0)
     pl.semaphore_wait(
         barrier, ROW - 1 + jnp.where(c > 0, 1, 0) + jnp.where(c < COL - 1, 1, 0)
     )
     for part in range(CHUNKS):
         if part > 0:
+            pair_loads[part].wait()
             norm_piece(part)
         chain_sends(c, part, False)
         source_sends(c, part, False)
 
-    for load in loads[3:]:
+    for load in loads[2:]:
         load.wait()
 
     def piece_rows(t):
@@ -351,7 +359,8 @@
             pltpu.VMEM((1, width), jnp.float32),
             pltpu.VMEM((1, width), jnp.float32),
             pltpu.VMEM(w_out.shape, jnp.bfloat16),
-            pltpu.SemaphoreType.DMA((10,)),
+            pltpu.SemaphoreType.DMA((9,)),
+            pltpu.SemaphoreType.DMA((CHUNKS,)),
             pltpu.VMEM((2 * COL, positions, width), jnp.bfloat16),
             pltpu.VMEM((positions, width), jnp.float32),
             pltpu.VMEM((8 * side, width), jnp.float32),

time: 40.9 us -> 41 us (level)
  no operation moved by 1% of the time
where the time goes in v4:
time: 41 us; the launch traced here: 40.8 us
  Pallas kernels  39 us (95%)
  local copies, waits for them, and re-layouts  1.79 us (4%)
    pallas_call x1, Pallas kernels, fused_shards(): pl.pallas_call(functools.partial(fused_kernel, side=side, slot_len=slot_l...  39 us
    unnamed x1, local copies, waits for them, and re-layouts  1.79 us

profile of v4, /device:TPU:0, one launch (start us, length us, event | category | flops | bytes accessed | tf_op | source)
XLA Modules:
  0.0 40.8 jit_solution(12328267523626436826)
XLA Ops:
  0.0 39.0 %shard_map.100 = bf16[1600,128]{1,0:T(8,128)(2,1)} custom-call(s32[4]{0:T(128)} %lengths_hbm.1, bf16[1600,128]{1,0:T(8,128)(2,1)} %bitcast.7, f32[1,128]{1,0:T(1,128)} %bitcast.8, f32[1,128]{1,0:T(1,128)} %bitcast.9, bf16[128,256]{1,0:T(8,128)(2,1)} %w_left_hbm.1, bf16[128,256]{1,0:T(8,128)(2,1)} %w_right_hbm.1, bf16[128,128]{1,0:T(8,128)(2,1)} %w_gate_hbm.1, ...), custom_call_target="tpu_custom_call" | custom-call | tf_op jit(solution)/shard_map/pallas_call | solution.py:346
  39.0 1.8 %copy.12 = bf16[40,40,128]{2,1,0:T(8,128)(2,1)} copy(bf16[40,40,128]{2,1,0:T(8,128)(2,1)} %bitcast.6) | data formatting | bytes 819200
